TPU v7x, 32 devices: a whole 2x2x4 slice. The times are simulated.
32 devices in a mesh: space: 16 (over z, y, x), sub: 2 (over core).
Axes of the slice: x: 2, y: 2, z: 4, core: 2. Of those that a mesh axis runs over, the one named last changes fastest.
Arguments:
- fields: bfloat16 [131072, 256], P(('space', 'sub')), may hold values from -6 to 6
- kriging: bfloat16 [512, 256, 768], P(('space', 'sub')), may hold values from -0.21875 to 0.21875
- whitening: bfloat16 [512, 256, 256], P(('space', 'sub')), may hold values from -0.375 to 0.375
- neighbours: int32 [512, 3], P(('space', 'sub')), may hold values from 0 to 511, as said below
- home: int32 [512], replicated, may hold values from 0 to 511, as said below
Outputs:
- gradient: bfloat16 [131072, 256], P(('space', 'sub'))
Inputs may be any that keep to these rules, and one draw needn't show every extreme that they name: `home`: A permutation of the slots that maps the block ids of every region onto that region's own slots. `neighbours`: the 3 x 16 references of one device name different blocks, none stored on that device. Each lies in the device's own region or in the region 1 or 2 before it along space, counting cyclically. At most 20 references of one device name blocks of one earlier region, and every device has exactly 20 towards one of its two earlier regions.
All inputs are finite; a program needn't handle non-finite values.
Results may differ from a plain program's by a relative error of at most 0.006.
Values may be sent and summed in bfloat16 or wider, within the bound.
A program may use at most 128 MiB of HBM per device.

v0:
```python
import jax
import jax.numpy as jnp
from jax import lax
from jax.sharding import PartitionSpec as P

REACH = 2
CAP = 20


def shifted(value, axis, steps):
    count = lax.axis_size(axis)
    pairs = [(source, (source + steps) % count) for source in range(count)]
    return lax.ppermute(value, axis, pairs)


def selector_for(distance, offset, capacity):
    wanted = distance == offset
    ranking = jnp.cumsum(wanted.astype(jnp.int32)) - 1
    places = jnp.arange(capacity, dtype=jnp.int32)
    return wanted[None, :] & (ranking[None, :] == places[:, None])


def body(fields, kriging, whitening, neighbours, home):
    block_count = kriging.shape[0]
    points = kriging.shape[1]
    order_size = kriging.shape[2]
    series = fields.shape[1]
    core_count = lax.axis_size("sub")
    region_count = lax.axis_size("space")
    region_size = block_count * core_count
    region_index = lax.axis_index("space")
    references = neighbours.reshape(-1)
    reference_count = references.shape[0]
    slot_ids = jnp.take(home, references)
    distance = (region_index - slot_ids // region_size) % region_count
    within = slot_ids % region_size
    gathered = lax.all_gather(fields, "sub", axis=0, tiled=True)
    region_view = gathered.reshape(region_size, points, series)
    selectors = []
    incomings = []
    picked = jnp.take(region_view, within, axis=0)
    for offset in range(1, REACH + 1):
        selector = selector_for(distance, offset, CAP)
        asked_ids = jnp.sum(jnp.where(selector, within[None, :], 0), axis=1)
        incoming = shifted(asked_ids, "space", -offset)
        served = jnp.take(region_view, incoming, axis=0)
        arrived = shifted(served, "space", offset)
        spread = jnp.dot(
            selector.T.astype(jnp.bfloat16),
            arrived.reshape(CAP, points * series),
            preferred_element_type=jnp.float32,
        )
        spread = spread.astype(jnp.bfloat16).reshape(reference_count, points, series)
        picked = jnp.where((distance == offset)[:, None, None], spread, picked)
        selectors.append(selector)
        incomings.append(incoming)
    neighbourhood = picked.reshape(block_count, order_size, series)
    own_fields = fields.reshape(block_count, points, series)
    prediction = jnp.einsum(
        "bpk,bks->bps", kriging, neighbourhood, preferred_element_type=jnp.float32
    )
    residual = (own_fields.astype(jnp.float32) - prediction).astype(jnp.bfloat16)
    whitened = jnp.einsum(
        "bpq,bqs->bps", whitening, residual, preferred_element_type=jnp.float32
    ).astype(jnp.bfloat16)
    pulled = jnp.einsum(
        "bqp,bqs->bps", whitening, whitened, preferred_element_type=jnp.float32
    ).astype(jnp.bfloat16)
    returned = jnp.einsum(
        "bpk,bps->bks", kriging, pulled, preferred_element_type=jnp.float32
    ).astype(jnp.bfloat16)
    returned = returned.reshape(reference_count, points, series)
    target = jnp.where(distance == 0, within, region_size)
    local_share = (
        jnp.zeros((region_size, points, series), jnp.bfloat16).at[target].set(returned, mode="drop")
    )
    region_total = local_share.astype(jnp.float32)
    for offset in range(1, REACH + 1):
        outgoing = jnp.dot(
            selectors[offset - 1].astype(jnp.bfloat16),
            returned.reshape(reference_count, points * series),
            preferred_element_type=jnp.float32,
        )
        outgoing = outgoing.astype(jnp.bfloat16).reshape(CAP, points, series)
        given_back = shifted(outgoing, "space", -offset)
        region_total = region_total.at[incomings[offset - 1]].add(given_back.astype(jnp.float32))
    own_sums = lax.psum_scatter(
        region_total.reshape(region_size * points, series), "sub", scatter_dimension=0, tiled=True
    )
    return (own_sums - pulled.reshape(block_count * points, series).astype(jnp.float32)).astype(
        jnp.bfloat16
    )


def solution(mesh):
    return jax.shard_map(
        body,
        mesh=mesh,
        in_specs=(
            P(("space", "sub"), None),
            P(("space", "sub"), None, None),
            P(("space", "sub"), None, None),
            P(("space", "sub"), None),
            P(),
        ),
        out_specs=P(("space", "sub"), None),
        check_vma=False,
    )
```

profile of v0, /device:TPU:2, one launch (start us, length us, event | category | flops | bytes accessed | tf_op | source)
XLA Modules:
  0.0 494.5 jit_solution(3357174691895485371)
XLA Ops:
  6.5 0.7 all-gather.2.cloned.1.call-update
  7.3 0.0 reduce-scatter.2.cloned.1.call-start
  7.3 0.8 copy.45
  8.1 0.1 reshape.530
  8.2 0.1 reshape.606
  8.2 0.1 fusion.16
  8.4 1.5 gather_fusion
  9.8 0.1 copy.49
  10.0 0.1 reduce-window.16
  10.1 0.1 reduce-window.17
  10.1 0.1 add_reduce_fusion
  10.3 0.1 select_reduce_fusion
  10.4 0.1 collective-permute-start.2
  10.5 5.1 %collective-permute-start = (s32[20]{0:T(128)S(1)}, s32[20]{0:T(128)S(1)}, u32[]{:S(2)}, u32[]{:S(2)}) collective-permute-start(s32[20]{0:T(128)S(1)} %get-tuple-element.9), channel_id=1, source_target_pairs={{0,28},{2,30},{4,0},{6,2},{8,4},{10,6},{12,8},{14,10},{16,12},{18,... | collective-permute-start | bytes 248 | tf_op jit(solution)/shard_map/ppermute | solution.py:13
  15.6 1.3 collective-permute-done
  16.9 7.2 %all-gather.2.cloned.1.call-done = bf16[8192,256]{1,0:T(8,128)(2,1)} async-done(((bf16[4096,256]{1,0:T(8,128)(2,1)}), bf16[8192,256]{1,0:T(8,128)(2,1)}) %all-gather.2.cloned.1.call-update) | async-done | bytes 4194320 | tf_op jit(solution)/shard_map/all_gather | solution.py:37
  24.1 4.6 gather_fusion.2
  28.7 4.5 gather_fusion.3
  33.2 3.7 broadcast_select_fusion
  36.9 1.5 collective-permute-start.3
  38.3 1.8 broadcast_select_fusion.1
  40.2 1.5 collective-permute-start.1
  41.6 0.1 gather.19
  41.8 0.1 broadcast_in_dim.101
  41.9 0.1 broadcast_in_dim.95
  42.0 0.1 broadcast_in_dim.104
  42.1 4.1 copy.55
  46.2 0.1 fusion.14
  46.4 7.2 %gather_fusion.1 = bf16[48,256,256]{2,1,0:T(8,128)(2,1)} fusion(bf16[32,256,256]{2,1,0:T(8,128)(2,1)} %bitcast.59, s32[1024]{0:T(1024)S(1)} %pad_clamp_fusion), kind=kCustom, calls=%fused_computation.3 | custom fusion | bytes 12583104 | tf_op jit(solution)/shard_map/jit(_take)/gather | solution.py:41
  53.5 42.7 %collective-permute-done.3 = bf16[20,256,256]{2,1,0:T(8,128)(2,1)} collective-permute-done((bf16[20,256,256]{2,1,0:T(8,128)(2,1)}, bf16[20,256,256]{2,1,0:T(8,128)(2,1)}, u32[]{:S(2)}, u32[]{:S(2)}) %collective-permute-start.3) | collective-permute-done | bytes 2621472 | tf_op jit(solution)/shard_map/ppermute | solution.py:13
  96.3 2.0 pad.5
  98.3 3.5 copy.66
  101.8 98.9 %collective-permute-done.1 = bf16[20,256,256]{2,1,0:T(8,128)(2,1)} collective-permute-done((bf16[20,256,256]{2,1,0:T(8,128)(2,1)}, bf16[20,256,256]{2,1,0:T(8,128)(2,1)}, u32[]{:S(2)}, u32[]{:S(2)}) %collective-permute-start.1) | collective-permute-done | bytes 2621472 | tf_op jit(solution)/shard_map/ppermute | solution.py:13
  200.7 2.0 pad.4
  202.8 1.8 copy.64
  204.5 4.6 convolution_convert_fusion.1
  209.2 8.1 %reshape.533 = bf16[16,768,256]{2,1,0:T(8,128)(2,1)} reshape(bf16[48,65536]{1,0:T(8,128)(2,1)} %convolution_convert_fusion.1) | data formatting | bytes 12582912 | tf_op jit(solution)/shard_map/reshape | solution.py:53
  217.3 6.4 %convolution_convert_fusion = bf16[48,65536]{1,0:T(8,128)(2,1)} fusion(bf16[20,65536]{1,0:T(8,128)(2,1)} %bitcast.61, s32[48]{0:T(128)S(1)} %get-tuple-element.18, pred[48]{0:T(512)(128)(4,1)S(1)} %broadcast_compare_fusion.3), kind=kOutput, calls=%fused_computation.7 | convolution fusion | flops 128976768 | bytes 8913136 | tf_op jit(solution)/shard_map/dot_general | solution.py:48
  223.7 8.1 %reshape.535 = bf16[16,768,256]{2,1,0:T(8,128)(2,1)} reshape(bf16[48,65536]{1,0:T(8,128)(2,1)} %convolution_convert_fusion) | data formatting | bytes 12582912 | tf_op jit(solution)/shard_map/reshape | solution.py:53
  231.8 9.6 %fusion.1 = bf16[16,768,256]{2,1,0:T(8,128)(2,1)} fusion(bf16[16,768,256]{2,1,0:T(8,128)(2,1)} %reshape.533, bf16[16,768,256]{2,1,0:T(8,128)(2,1)} %reshape.535, pred[16,768]{1,0:T(8,128)(4,1)S(1)} %bitcast.75, pred[16,768]{1,0:T(8,128)(4,1)S(1)} %bitcast.73, pred[16,768]{1,0:T(8,128)(4,1)S(1)} %bitcast.74, bf16[16,768,256]{2,1,0:T(8,128)(2,1)} %bitcast.60), kind=kLoop, calls=%fused_computation.13 | loop fusion | flops 9437184 | bytes 25202688 | tf_op jit(solution)/shard_map/jit(_where)/select_n | solution.py:54
  241.4 9.1 %fusion.3 = bf16[16,256,256]{1,2,0:T(8,128)(2,1)} fusion(f32[16,256,256]{1,2,0:T(8,128)} %copy.55, bf16[16,768,256]{2,1,0:T(8,128)(2,1)} %fusion.1, bf16[16,256,768]{2,1,0:T(8,128)(2,1)} %param.8), kind=kOutput, calls=%fused_computation.18 | convolution fusion | flops 1612709888 | bytes 18874368 | tf_op jit(solution)/shard_map/bpk,bks->bps/dot_general | solution.py:59
  250.4 4.3 fusion.8
  254.7 8.0 %convert_bitcast_fusion = bf16[16,768,256]{1,2,0:T(8,128)(2,1)} fusion(bf16[16,256,256]{1,2,0:T(8,128)(2,1)} %fusion.8, bf16[16,256,768]{2,1,0:T(8,128)(2,1)} %param.8), kind=kOutput, calls=%fused_computation.14 | convolution fusion | flops 1613758464 | bytes 14680064 | tf_op jit(solution)/shard_map/bpk,bps->bks/dot_general | solution.py:69
  262.7 8.7 %copy.58 = bf16[16,768,256]{2,1,0:T(8,128)(2,1)} copy(bf16[16,768,256]{1,2,0:T(8,128)(2,1)} %convert_bitcast_fusion) | data formatting | bytes 12582912 | tf_op jit(solution)/shard_map/convert_element_type | solution.py:71
  271.4 8.1 %reshape_reshape.4 = bf16[48,65536]{1,0:T(8,128)(2,1)} reshape(bf16[16,768,256]{2,1,0:T(8,128)(2,1)} %copy.58) | data formatting | bytes 12582912 | tf_op jit(solution)/shard_map/reshape;reshape | solution.py:81
  279.4 3.9 convolution_convert_fusion.2
  283.3 0.7 copy-done.2
  284.0 1.0 convolution_convert_fusion.3
  285.0 0.7 copy.68
  285.7 1.7 slice.8
  287.4 0.7 copy.69
  288.2 0.1 collective-permute-start.4
  288.2 1.7 slice.9
  289.9 2.4 broadcast_in_dim.92
  292.4 15.9 %scatter_fusion = bf16[32,256,256]{2,1,0:T(8,128)(2,1)} fusion(bf16[32,256,256]{2,1,0:T(8,128)(2,1)} %broadcast_in_dim.92, s32[48]{0:T(128)S(1)} %get-tuple-element.7, bf16[48,256,256]{2,1,0:T(8,128)(2,1)} %bitcast.56), kind=kCustom, calls=%fused_computation.4 | custom fusion | bytes 18874560 | tf_op jit(solution)/shard_map/scatter | solution.py:75
  308.2 6.6 %convert_element_type.95 = f32[32,256,256]{2,1,0:T(8,128)} convert(bf16[32,256,256]{2,1,0:T(8,128)(2,1)} %scatter_fusion) | non-fusion elementwise | flops 2097152 | bytes 12582912 | tf_op jit(solution)/shard_map/convert_element_type | solution.py:77
  314.8 32.9 %collective-permute-done.4 = bf16[20,256,256]{2,1,0:T(8,128)(2,1)} collective-permute-done((bf16[20,256,256]{2,1,0:T(8,128)(2,1)}, bf16[20,256,256]{2,1,0:T(8,128)(2,1)}, u32[]{:S(2)}, u32[]{:S(2)}) %collective-permute-start.4) | collective-permute-done | bytes 2621472 | tf_op jit(solution)/shard_map/ppermute | solution.py:13
  347.8 4.7 convert_element_type.97
  352.4 13.7 %scatter_fusion.1 = f32[32,256,256]{2,1,0:T(8,128)} fusion(f32[32,256,256]{2,1,0:T(8,128)} %convert_element_type.95, s32[20]{0:T(128)S(1)} %compare_select_fusion.5, f32[20,256,256]{2,1,0:T(8,128)} %convert_element_type.97), kind=kCustom, calls=%fused_computation.5 | custom fusion | flops 1310720 | bytes 15728720 | tf_op jit(solution)/shard_map/scatter-add | solution.py:86
  366.1 37.7 %collective-permute-done.5 = bf16[20,256,256]{2,1,0:T(8,128)(2,1)} collective-permute-done((bf16[20,256,256]{2,1,0:T(8,128)(2,1)}, bf16[20,256,256]{2,1,0:T(8,128)(2,1)}, u32[]{:S(2)}, u32[]{:S(2)}) %collective-permute-start.5) | collective-permute-done | bytes 2621472 | tf_op jit(solution)/shard_map/ppermute | solution.py:13
  403.8 4.6 convert_element_type.99
  408.4 13.6 %scatter_fusion.2 = f32[32,256,256]{2,1,0:T(8,128)} fusion(f32[32,256,256]{2,1,0:T(8,128)} %scatter_fusion.1, s32[20]{0:T(128)S(1)} %compare_select_fusion.6, f32[20,256,256]{2,1,0:T(8,128)} %convert_element_type.99), kind=kCustom, calls=%fused_computation.6 | custom fusion | flops 1310720 | bytes 15728720 | tf_op jit(solution)/shard_map/scatter-add | solution.py:86
  422.0 60.9 %reduce-scatter.2.cloned.1.call-done = f32[4096,256]{1,0:T(8,128)} async-done(((f32[8192,256]{1,0:T(8,128)}), f32[4096,256]{1,0:T(8,128)}) %reduce-scatter.2.cloned.1.call-update) | async-done | bytes 4194320 | tf_op jit(solution)/shard_map/reduce_scatter | solution.py:87
  483.0 4.7 fusion.2
  (29 shorter events, 0.2 us)
Async XLA Ops:
  6.5 243.9 %copy-start = (bf16[16,256,256]{2,1,0:T(8,128)(2,1)S(1)}, bf16[16,256,256]{2,1,0:T(8,128)(2,1)}, u32[]{:S(2)}) copy-start(bf16[16,256,256]{2,1,0:T(8,128)(2,1)} %param.9) | copy-start | bytes 6291460
  6.5 17.6 %all-gather.2.cloned.1.call-start = ((), (), s32[]{:S(2)}) async-start(), calls=%async_computation.1 | async-start | bytes 6291456 | tf_op jit(solution)/shard_map/all_gather | solution.py:37
  7.3 475.7 %reduce-scatter.2.cloned.1.call-start = ((), (), s32[]{:S(2)}) async-start(), calls=%async_computation.2 | async-start | bytes 12582912 | tf_op jit(solution)/shard_map/reduce_scatter | solution.py:87
  10.4 5.1 %collective-permute-start.2 = (s32[20]{0:T(128)S(1)}, s32[20]{0:T(128)S(1)}, u32[]{:S(2)}, u32[]{:S(2)}) collective-permute-start(s32[20]{0:T(128)S(1)} %get-tuple-element.8), channel_id=1, source_target_pairs={{0,30},{2,0},{4,2},{6,4},{8,6},{10,8},{12,10},{14,12},{16,14},{18,... | collective-permute-start | bytes 248 | tf_op jit(solution)/shard_map/ppermute | solution.py:13
  10.5 6.4 %collective-permute-start = (s32[20]{0:T(128)S(1)}, s32[20]{0:T(128)S(1)}, u32[]{:S(2)}, u32[]{:S(2)}) collective-permute-start(s32[20]{0:T(128)S(1)} %get-tuple-element.9), channel_id=1, source_target_pairs={{0,28},{2,30},{4,0},{6,2},{8,4},{10,6},{12,8},{14,10},{16,12},{18,... | collective-permute-start | bytes 248 | tf_op jit(solution)/shard_map/ppermute | solution.py:13
  33.2 5.2 %copy-start.3 = (bf16[20,256,256]{2,1,0:T(8,128)(2,1)S(1)}, bf16[20,256,256]{2,1,0:T(8,128)(2,1)}, u32[]{:S(2)}) copy-start(bf16[20,256,256]{2,1,0:T(8,128)(2,1)} %gather_fusion.2) | copy-start | bytes 7864324
  36.9 59.4 %collective-permute-start.3 = (bf16[20,256,256]{2,1,0:T(8,128)(2,1)}, bf16[20,256,256]{2,1,0:T(8,128)(2,1)}, u32[]{:S(2)}, u32[]{:S(2)}) collective-permute-start(bf16[20,256,256]{2,1,0:T(8,128)(2,1)} %broadcast_select_fusion), channel_id=1, source_target_pairs={{0,2},{2,4},{4,6},{6,8},{8,10},{10,12},{12,14},{14,16},{16,18},{18... | collective-permute-start | bytes 7864328 | tf_op jit(solution)/shard_map/ppermute | solution.py:13
  40.2 160.5 %collective-permute-start.1 = (bf16[20,256,256]{2,1,0:T(8,128)(2,1)}, bf16[20,256,256]{2,1,0:T(8,128)(2,1)}, u32[]{:S(2)}, u32[]{:S(2)}) collective-permute-start(bf16[20,256,256]{2,1,0:T(8,128)(2,1)} %broadcast_select_fusion.1), channel_id=1, source_target_pairs={{0,4},{2,6},{4,8},{6,10},{8,12},{10,14},{12,16},{14,18},{16,20},{1... | collective-permute-start | bytes 7864328 | tf_op jit(solution)/shard_map/ppermute | solution.py:13
  279.4 4.6 copy-start.2
  288.2 59.6 %collective-permute-start.4 = (bf16[20,256,256]{2,1,0:T(8,128)(2,1)}, bf16[20,256,256]{2,1,0:T(8,128)(2,1)}, u32[]{:S(2)}, u32[]{:S(2)}) collective-permute-start(bf16[20,256,256]{2,1,0:T(8,128)(2,1)} %slice.8), channel_id=1, source_target_pairs={{0,30},{2,0},{4,2},{6,4},{8,6},{10,8},{12,10},{14,12},{16,14},{18,... | collective-permute-start | bytes 7864328 | tf_op jit(solution)/shard_map/ppermute | solution.py:13
  289.9 113.9 %collective-permute-start.5 = (bf16[20,256,256]{2,1,0:T(8,128)(2,1)}, bf16[20,256,256]{2,1,0:T(8,128)(2,1)}, u32[]{:S(2)}, u32[]{:S(2)}) collective-permute-start(bf16[20,256,256]{2,1,0:T(8,128)(2,1)} %slice.9), channel_id=1, source_target_pairs={{0,28},{2,30},{4,0},{6,2},{8,4},{10,6},{12,8},{14,10},{16,12},{18,... | collective-permute-start | bytes 7864328 | tf_op jit(solution)/shard_map/ppermute | solution.py:13
  422.0 65.6 %copy-start.1 = (bf16[16,256,256]{2,1,0:T(8,128)(2,1)S(1)}, bf16[16,256,256]{2,1,0:T(8,128)(2,1)}, u32[]{:S(2)}) copy-start(bf16[16,256,256]{2,1,0:T(8,128)(2,1)} %param.9) | copy-start | bytes 6291460
Sparse Core Ops, SparseCore 0:
  8.9 15.1 all-gather.1
  422.2 60.7 reduce-scatter.1
where the time goes:
time: 497 us; the launch traced here: 494 us
  waiting for transfers between devices  282 us (57%)
  local copies, waits for them, and re-layouts  89.4 us (18%)
  other arithmetic  63.7 us (13%)
  matrix products  37.2 us (7%)
  between operations  13.6 us (3%)
  starting transfers between devices  8.18 us (2%)
    ppermute x6, waiting for transfers between devices, shifted(): return lax.ppermute(value, axis, pairs)  214 us
    reduce_scatter x1, waiting for transfers between devices, body(): lax.psum_scatter(region_total.reshape(region_size * points, series), 'sub...  60.9 us
    scatter-add x2, other arithmetic, body(): region_total.at[incomings[offset - 1]].add(given_back.astype(jnp.float32))  27.3 us
    reshape x2, local copies, waits for them, and re-layouts, body(): spread.astype(jnp.bfloat16).reshape(reference_count, points, series)  16.2 us
    scatter x1, local copies, waits for them, and re-layouts, body(): jnp.zeros((region_size, points, series), jnp.bfloat16).at[target]  15.9 us
    unnamed x18, local copies, waits for them, and re-layouts  12.3 us
    dot_general x2, matrix products, body(): jnp.dot(selector.T.astype(jnp.bfloat16), arrived.reshape(CAP, points * se...  11 us
  transfers between devices with their start and end apart: 8, of which 7 were waited for; matrix products, arithmetic and copies ran while one was open for 14% of the time, Pallas kernels for 0%

commit v1 on v0

v1 whole, which is shorter than its diff:
```python
import functools

import jax
import jax.numpy as jnp
from jax import lax
from jax.experimental import pallas as pl
from jax.experimental.pallas import tpu as pltpu
from jax.sharding import PartitionSpec as P

MESH = pl.DeviceIdType.MESH
F32 = jnp.float32
BF16 = jnp.bfloat16
CHUNK = 1
PAIR = 2


def kernel(
    regions,
    fields, kriging, whitening, neighbours, home,
    out,
    held, krig, white, krig_t, white_t, back, pulled, swapped, landed, places, inverse,
    load_sem, near_s, near_r, far_s, far_r, own_s, own_r, pass_s, pass_r,
    swap_s, swap_r, low_s, low_r, deep_s, deep_r, out_sem,
):
    blocks, points, _ = fields.shape
    region = 2 * blocks
    width = kriging.shape[2] // points
    refs = blocks * width
    steps = blocks // CHUNK
    me = lax.axis_index("space")
    core = lax.axis_index("sub")
    other = 1 - core
    parity = lax.rem(me, 2)
    even = parity == 0
    flip = me + 1 - 2 * parity
    ahead = lax.rem(me + 2, regions)
    behind = lax.rem(me + regions - 2, regions)
    partner = (me, other)
    mine = core * blocks
    theirs = other * blocks

    def send(src, dst, ssem, rsem, device):
        return pltpu.make_async_remote_copy(
            src_ref=src, dst_ref=dst, send_sem=ssem, recv_sem=rsem, device_id=device, device_id_type=MESH
        )

    def piece(ref, base, i):
        return ref.at[pl.ds(base + i * CHUNK, CHUNK)]

    def far(i):
        return send(piece(fields, 0, i), piece(held, 2 * region + mine, i), far_s.at[i], far_r.at[i], (ahead, core))

    def near(i):
        return send(piece(fields, 0, i), piece(held, region + mine, i), near_s.at[i], near_r.at[i], (flip, core))

    def near_relay(i):
        return send(
            piece(held, 2 * region + mine, i), piece(held, region + mine, i), near_s.at[i], near_r.at[i], (flip, core)
        )

    def own(half):
        return send(fields, held.at[pl.ds(half, blocks)], own_s, own_r, partner)

    def handed(which, half, i):
        spot = piece(held, which * region + half, i)
        k = (which - 1) * steps + i
        return send(spot, spot, pass_s.at[k], pass_r.at[k], partner)

    barrier = pltpu.get_barrier_semaphore()
    for device in (partner, (flip, core), (ahead, core), (behind, core)):
        pl.semaphore_signal(barrier, inc=1, device_id=device, device_id_type=MESH)
    pl.semaphore_wait(barrier, 4)

    @pl.loop(0, steps)
    def _(i):
        far(i).start()

        @pl.when(even)
        def _():
            near(i).start()

    load_w = pltpu.make_async_copy(whitening, white, load_sem.at[0])
    load_k = pltpu.make_async_copy(kriging, krig, load_sem.at[1])
    load_f = pltpu.make_async_copy(fields, held.at[pl.ds(mine, blocks)], load_sem.at[2])
    load_w.start()
    load_k.start()
    load_f.start()
    own(mine).start()

    back[refs] = jnp.zeros((points, fields.shape[2]), BF16)

    @pl.loop(0, blocks)
    def _(b):
        for k in range(width):
            slot = home[neighbours[b, k]]
            whose = slot // region
            distance = me - whose
            distance = jnp.where(distance < 0, distance + regions, distance)
            distance = jnp.minimum(distance, 2)
            places[b * width + k] = distance * region + slot - whose * region

    load_w.wait()
    load_k.wait()
    load_f.wait()
    targets = 3 * region // steps

    @pl.loop(0, steps)
    def _(i):
        far(i).wait_recv()

        @pl.when(parity == 1)
        def _():
            near_relay(i).start()

        handed(2, mine, i).start()

        for d in range(CHUNK):
            b = i * CHUNK + d
            white_t[b] = white[b].T
            for k in range(width):
                krig_t[b * width + k] = krig[b, :, k * points : (k + 1) * points].T

        @pl.loop(0, targets)
        def _(u):
            t = i * targets + u
            found = jnp.int32(refs)
            for j in range(refs):
                found = jnp.where(places[j] == t, j, found)
            inverse[t] = found

        near(i).wait_recv()
        handed(1, mine, i).start()

    own(theirs).wait_recv()

    @pl.loop(0, steps)
    def _(i):
        handed(2, theirs, i).wait_recv()
        handed(1, theirs, i).wait_recv()

    def dot(a, b):
        return jnp.dot(a, b, preferred_element_type=F32)

    @pl.loop(0, blocks // PAIR)
    def _(g):
        group = [g * PAIR + d for d in range(PAIR)]
        preds = []
        for b in group:
            total = None
            for k in range(width):
                term = dot(krig[b, :, k * points : (k + 1) * points], held[places[b * width + k]])
                total = term if total is None else total + term
            preds.append(total)
        rests = [(held[mine + b].astype(F32) - p).astype(BF16) for b, p in zip(group, preds)]
        whites = [dot(white[b], r).astype(BF16) for b, r in zip(group, rests)]
        pulls = [dot(white_t[b], w).astype(BF16) for b, w in zip(group, whites)]
        for b, p in zip(group, pulls):
            pulled[b] = p
        for b, p in zip(group, pulls):
            for k in range(width):
                back[b * width + k] = dot(krig_t[b * width + k], p).astype(BF16)

    own(mine).wait_send()

    @pl.loop(0, steps)
    def _(i):
        far(i).wait_send()
        near(i).wait_send()
        handed(2, mine, i).wait_send()
        handed(1, mine, i).wait_send()

    def swap(which, i):
        k = which * steps + i
        return send(
            piece(held, which * blocks, i), piece(swapped, which * blocks, i), swap_s.at[k], swap_r.at[k], partner
        )

    def offer(which, i):
        for d in range(CHUNK):
            t = i * CHUNK + d
            held[which * blocks + t] = back[inverse[which * region + theirs + t]]
        swap(which, i).start()

    sums = 3 * blocks

    def low(i):
        return send(piece(held, sums, i), piece(landed, 0, i), low_s.at[i], low_r.at[i], (flip, core))

    def deep(i):
        return send(
            piece(held, sums + blocks, i), piece(landed, blocks, i), deep_s.at[i], deep_r.at[i], (behind, core)
        )

    def add_low(i):
        swap(1, i).wait_recv()
        for d in range(CHUNK):
            t = i * CHUNK + d
            total = back[inverse[region + mine + t]].astype(F32) + swapped[blocks + t].astype(F32)
            held[sums + t] = total.astype(BF16)
        low(i).start()

    def add_deep(i, relay):
        swap(2, i).wait_recv()
        if relay:
            low(i).wait_recv()
        for d in range(CHUNK):
            t = i * CHUNK + d
            total = back[inverse[2 * region + mine + t]].astype(F32) + swapped[2 * blocks + t].astype(F32)
            if relay:
                total = total + landed[t].astype(F32)
            held[sums + blocks + t] = total.astype(BF16)
        deep(i).start()

    @pl.loop(0, steps)
    def _(i):
        offer(1, i)
        offer(2, i)

    @pl.when(even)
    def _():
        @pl.loop(0, steps)
        def _(i):
            add_low(i)
            add_deep(i, False)

    @pl.when(parity == 1)
    def _():
        @pl.loop(0, steps)
        def _(i):
            add_low(i)

    @pl.loop(0, steps)
    def _(i):
        offer(0, i)

    @pl.when(parity == 1)
    def _():
        @pl.loop(0, steps)
        def _(i):
            add_deep(i, True)

    results = sums + 2 * blocks

    def store(i):
        return pltpu.make_async_copy(piece(held, results, i), piece(out, 0, i), out_sem.at[i])

    @pl.loop(0, steps)
    def _(i):
        swap(0, i).wait_recv()

        @pl.when(even)
        def _():
            low(i).wait_recv()

        deep(i).wait_recv()
        for d in range(CHUNK):
            t = i * CHUNK + d
            total = swapped[t].astype(F32) - pulled[t].astype(F32) + landed[blocks + t].astype(F32)
            total = total + jnp.where(even, landed[t].astype(F32), 0.0)
            held[results + t] = total.astype(BF16)
        store(i).start()

    @pl.loop(0, steps)
    def _(i):
        for which in range(3):
            swap(which, i).wait_send()
        low(i).wait_send()
        deep(i).wait_send()
        store(i).wait()


def body(regions, fields, kriging, whitening, neighbours, home):
    blocks, points, order = kriging.shape
    series = fields.shape[1]
    region = 2 * blocks
    refs = neighbours.size
    steps = blocks // CHUNK
    any_space = pl.BlockSpec(memory_space=pl.ANY)
    smem = pl.BlockSpec(memory_space=pltpu.SMEM)
    dma = pltpu.SemaphoreType.DMA

    def rows(count):
        return pltpu.VMEM((count, points, series), BF16)

    result = pl.pallas_call(
        functools.partial(kernel, regions),
        out_shape=jax.ShapeDtypeStruct((blocks, points, series), BF16),
        in_specs=[any_space, any_space, any_space, smem, smem],
        out_specs=any_space,
        scratch_shapes=[
            rows(3 * region),
            pltpu.VMEM((blocks, points, order), BF16),
            pltpu.VMEM((blocks, points, points), BF16),
            pltpu.VMEM((refs, points, points), BF16),
            pltpu.VMEM((blocks, points, points), BF16),
            rows(refs + 1),
            rows(blocks),
            rows(3 * blocks),
            rows(2 * blocks),
            pltpu.SMEM((refs,), jnp.int32),
            pltpu.SMEM((3 * region,), jnp.int32),
            dma((3,)),
            dma((steps,)), dma((steps,)), dma((steps,)), dma((steps,)),
            dma, dma,
            dma((2 * steps,)), dma((2 * steps,)),
            dma((3 * steps,)), dma((3 * steps,)),
            dma((steps,)), dma((steps,)), dma((steps,)), dma((steps,)),
            dma((steps,)),
        ],
        compiler_params=pltpu.CompilerParams(
            collective_id=0, has_side_effects=True, vmem_limit_bytes=56 * 1024 * 1024
        ),
        cost_estimate=pl.CostEstimate(
            flops=4 * blocks * points * series * (order + points),
            bytes_accessed=2 * (kriging.size + whitening.size + 2 * fields.size),
            transcendentals=0,
        ),
    )(fields.reshape(blocks, points, series), kriging, whitening, neighbours, home)
    return result.reshape(blocks * points, series)


def solution(mesh):
    return jax.shard_map(
        functools.partial(body, mesh.shape["space"]),
        mesh=mesh,
        in_specs=(
            P(("space", "sub"), None),
            P(("space", "sub"), None, None),
            P(("space", "sub"), None, None),
            P(("space", "sub"), None),
            P(),
        ),
        out_specs=P(("space", "sub"), None),
        check_vma=False,
    )
```

time: 497 us -> 128 us (0.26)
  waiting for transfers between devices: 282 us -> 0 us
  Pallas kernels: 0 us -> 123 us
  local copies, waits for them, and re-layouts: 89.4 us -> 4.4 us
  other arithmetic: 63.7 us -> 0 us
  matrix products: 37.2 us -> 0 us
  between operations: 13.6 us -> 0.01 us
  starting transfers between devices: 8.18 us -> 0 us
    ppermute x6 -> x0, waiting for transfers between devices: 214 us -> none  [shifted(): return lax.ppermute(value, axis, pairs)]
    pallas_call x0 -> x1, Pallas kernels: none -> 123 us  [body(): pl.pallas_call(functools.partial(kernel, regions), out_shape=jax.ShapeDty...]
    reduce_scatter x1 -> x0, waiting for transfers between devices: 60.9 us -> none  [body(): lax.psum_scatter(region_total.reshape(region_size * points, series), 'sub...]
    dot_general x7 -> x0, matrix products: 37.2 us -> none  [the longest x2 11 us: body(): jnp.dot(selector.T.astype(jnp.bfloat16), arrived.reshape(CAP, points * se...]
    scatter-add x2 -> x0, other arithmetic: 27.3 us -> none  [body(): region_total.at[incomings[offset - 1]].add(given_back.astype(jnp.float32))]
    convert_element_type x6 -> x0, other arithmetic: 20.6 us -> none  [the longest x2 9.27 us: body(): given_back.astype(jnp.float32)]
    reshape x6 -> x0, local copies, waits for them, and re-layouts: 19.8 us -> none  [the longest x2 16.2 us: body(): spread.astype(jnp.bfloat16).reshape(reference_count, points, series)]
    gather x6 -> x0, local copies, waits for them, and re-layouts: 17.9 us -> none  [the longest x2 9.09 us: body(): served = jnp.take(region_view, incoming, axis=0)]
  transfers between devices with their start and end apart: 8 -> 0, of which waited for: 7 -> 0; matrix products, arithmetic and copies ran while one was open for 14% -> 0% of each run, Pallas kernels for 0% -> 0%
where the time goes in v1:
time: 128 us
  Pallas kernels  123 us (96%)
  local copies, waits for them, and re-layouts  4.4 us (3%)
    pallas_call x1, Pallas kernels, body(): pl.pallas_call(functools.partial(kernel, regions), out_shape=jax.ShapeDty...  123 us
    unnamed x2, local copies, waits for them, and re-layouts  4.4 us

profile of v1, /device:TPU:2, one launch (start us, length us, event | category | flops | bytes accessed | tf_op | source)
XLA Modules:
  0.0 127.7 jit_solution(5313568027287750614)
XLA Ops:
  0.0 1.4 %copy.6.neighbours = s32[16,3]{1,0:T(8,128)} copy(s32[16,3]{0,1:T(4,128)} %param.8) | data formatting | bytes 384 | tf_op args[3]
  1.4 123.3 %shard_map.55 = bf16[16,256,256]{2,1,0:T(8,128)(2,1)} custom-call(bf16[16,256,256]{2,1,0:T(8,128)(2,1)} %bitcast.3, bf16[16,256,768]{2,1,0:T(8,128)(2,1)} %kriging.1, bf16[16,256,256]{2,1,0:T(8,128)(2,1)} %whitening.1, s32[16,3]{1,0:T(8,128)} %copy.6.neighbours, s32[512]{0:T(512)} %home.1), custom_call_target="tpu_custom_call" | custom-call | flops 4294967296 | bytes 12582912 | tf_op jit(solution)/shard_map/pallas_call | solution.py:285
  124.7 3.0 %copy.8 = bf16[4096,256]{1,0:T(8,128)(2,1)} copy(bf16[4096,256]{1,0:T(8,128)(2,1)} %bitcast.2) | data formatting | bytes 4194304

commit v2 on v1

v2 whole, which is shorter than its diff:
```python
import functools

import jax
import jax.numpy as jnp
from jax import lax
from jax.experimental import pallas as pl
from jax.experimental.pallas import tpu as pltpu
from jax.sharding import PartitionSpec as P

MESH = pl.DeviceIdType.MESH
F32 = jnp.float32
BF16 = jnp.bfloat16
CHUNK = 2
WINDOW = 4


def kernel(
    regions,
    fields, kriging, whitening, neighbours, home,
    out,
    held_a, held_b, krig, white, krig_t, white_t, back_a, back_b, pulled, swapped, landed, places, inverse,
    load_sem, near_s, near_r, far_s, far_r, own_s, own_r, pass_s, pass_r,
    swap_s, swap_r, low_s, low_r, deep_s, deep_r, out_sem,
):
    held = (held_a, held_b)
    swapped = (swapped.at[0], swapped.at[1])
    landed = (landed.at[0], landed.at[1])
    pulled = (pulled.at[0], pulled.at[1])
    back = (back_a, back_b)
    blocks, points, series = fields.shape
    cols = series // 2
    region = 2 * blocks
    width = kriging.shape[2] // points
    refs = blocks * width
    steps = blocks // CHUNK
    half_steps = steps // 2
    me = lax.axis_index("space")
    core = lax.axis_index("sub")
    other = 1 - core
    parity = lax.rem(me, 2)
    even = parity == 0
    odd = parity == 1
    flip = me + 1 - 2 * parity
    ahead = lax.rem(me + 2, regions)
    behind = lax.rem(me + regions - 2, regions)
    partner = (me, other)
    mine = core * blocks
    theirs = other * blocks

    def send(src, dst, ssem, rsem, device):
        return pltpu.make_async_remote_copy(
            src_ref=src, dst_ref=dst, send_sem=ssem, recv_sem=rsem, device_id=device, device_id_type=MESH
        )

    def piece(ref, h, base, i):
        return ref[h].at[pl.ds(base + i * CHUNK, CHUNK)]

    def far(h, i):
        k = h * steps + i
        return send(
            piece(held, h, mine, i), piece(held, h, 2 * region + mine, i), far_s.at[k], far_r.at[k], (ahead, core)
        )

    def near(h, i, start):
        k = h * steps + i
        return send(
            piece(held, h, start + mine, i), piece(held, h, region + mine, i),
            near_s.at[k], near_r.at[k], (flip, core),
        )

    def own(h, half):
        spot = held[h].at[pl.ds(half, blocks)]
        return send(spot, spot, own_s.at[h], own_r.at[h], partner)

    def handed(h, which, half, i):
        spot = piece(held, h, which * region + half, i)
        k = (h * 2 + which - 1) * steps + i
        return send(spot, spot, pass_s.at[k], pass_r.at[k], partner)

    def load_fields(h):
        return pltpu.make_async_copy(
            fields.at[:, :, pl.ds(h * cols, cols)], held[h].at[pl.ds(mine, blocks)], load_sem.at[2 + h]
        )

    load_w = pltpu.make_async_copy(whitening, white, load_sem.at[0])
    load_k = pltpu.make_async_copy(kriging, krig, load_sem.at[1])
    load_fields(0).start()
    load_fields(1).start()
    load_w.start()
    load_k.start()

    barrier = pltpu.get_barrier_semaphore()
    for device in (partner, (flip, core), (ahead, core), (behind, core)):
        pl.semaphore_signal(barrier, inc=1, device_id=device, device_id_type=MESH)
    pl.semaphore_wait(barrier, 4)

    def start_own(h, i):
        far(h, i).start()

        @pl.when(even)
        def _():
            near(h, i, 0).start()

    load_fields(0).wait()
    for i in range(WINDOW):
        start_own(0, i)
    own(0, mine).start()
    load_fields(1).wait()
    own(1, mine).start()

    for h in range(2):
        back[h][refs] = jnp.zeros((points, cols), BF16)

    @pl.loop(0, blocks)
    def _(b):
        for k in range(width):
            slot = home[neighbours[k, b]]
            whose = slot // region
            distance = me - whose
            distance = jnp.where(distance < 0, distance + regions, distance)
            distance = jnp.minimum(distance, 2)
            places[b * width + k] = distance * region + slot - whose * region

    load_w.wait()
    load_k.wait()
    targets = 3 * region // steps

    def relay(h, i):
        far(h, i).wait_recv()

        @pl.when(odd)
        def _():
            near(h, i, 2 * region).start()

        handed(h, 2, mine, i).start()

    def relay_near(h, i):
        near(h, i, 0).wait_recv()
        handed(h, 1, mine, i).start()

    def arrived(h):
        own(h, theirs).wait_recv()

        @pl.loop(0, steps)
        def _(i):
            handed(h, 2, theirs, i).wait_recv()
            handed(h, 1, theirs, i).wait_recv()

    def sent(h):
        own(h, mine).wait_send()

        @pl.loop(0, steps)
        def _(i):
            far(h, i).wait_send()
            near(h, i, 0).wait_send()
            handed(h, 2, mine, i).wait_send()
            handed(h, 1, mine, i).wait_send()

    def dot(a, b):
        return jnp.dot(a, b, preferred_element_type=F32)

    def compute(h, g):
        group = [g * CHUNK + d for d in range(CHUNK)]
        preds = []
        for b in group:
            total = None
            for k in range(width):
                term = dot(krig[b, :, k * points : (k + 1) * points], held[h][places[b * width + k]])
                total = term if total is None else total + term
            preds.append(total)
        rests = [(held[h][mine + b].astype(F32) - p).astype(BF16) for b, p in zip(group, preds)]
        whites = [dot(white[b], r).astype(BF16) for b, r in zip(group, rests)]
        pulls = [dot(white_t[b], w).astype(BF16) for b, w in zip(group, whites)]
        for b, p in zip(group, pulls):
            pulled[h][b] = p
        for b, p in zip(group, pulls):
            for k in range(width):
                back[h][b * width + k] = dot(krig_t[b * width + k], p).astype(BF16)

    def swap(h, which, i):
        k = (h * 3 + which) * steps + i
        return send(
            piece(held, h, which * blocks, i), piece(swapped, h, which * blocks, i),
            swap_s.at[k], swap_r.at[k], partner,
        )

    def offer(h, which, i):
        for d in range(CHUNK):
            t = i * CHUNK + d
            held[h][which * blocks + t] = back[h][inverse[which * region + theirs + t]]
        swap(h, which, i).start()

    sums = 3 * blocks
    results = sums + 2 * blocks

    def low(h, i):
        k = h * steps + i
        return send(piece(held, h, sums, i), piece(landed, h, 0, i), low_s.at[k], low_r.at[k], (flip, core))

    def deep(h, i):
        k = h * steps + i
        return send(
            piece(held, h, sums + blocks, i), piece(landed, h, blocks, i), deep_s.at[k], deep_r.at[k], (behind, core)
        )

    def add_low(h, i):
        swap(h, 1, i).wait_recv()
        for d in range(CHUNK):
            t = i * CHUNK + d
            total = back[h][inverse[region + mine + t]].astype(F32) + swapped[h][blocks + t].astype(F32)
            held[h][sums + t] = total.astype(BF16)
        low(h, i).start()

    def add_deep(h, i, relayed):
        swap(h, 2, i).wait_recv()
        if relayed:
            low(h, i).wait_recv()
        for d in range(CHUNK):
            t = i * CHUNK + d
            total = back[h][inverse[2 * region + mine + t]].astype(F32) + swapped[h][2 * blocks + t].astype(F32)
            if relayed:
                total = total + landed[h][t].astype(F32)
            held[h][sums + blocks + t] = total.astype(BF16)
        deep(h, i).start()

    def add(h, i):
        add_low(h, i)

        @pl.when(even)
        def _():
            add_deep(h, i, False)

    def return_step(h, q):
        for e in range(2):
            offer(h, 1, 2 * q + e)
            offer(h, 2, 2 * q + e)

        @pl.when(q > 0)
        def _():
            for e in range(2):
                add(h, 2 * q - 2 + e)

    def return_end(h):
        for e in range(2):
            add(h, steps - 2 + e)

    def store(h, i):
        return pltpu.make_async_copy(
            piece(held, h, results, i),
            out.at[pl.ds(i * CHUNK, CHUNK), :, pl.ds(h * cols, cols)],
            out_sem.at[h * steps + i],
        )

    def finish(h, i):
        swap(h, 0, i).wait_recv()

        @pl.when(even)
        def _():
            low(h, i).wait_recv()

        deep(h, i).wait_recv()
        for d in range(CHUNK):
            t = i * CHUNK + d
            total = swapped[h][t].astype(F32) - pulled[h][t].astype(F32) + landed[h][blocks + t].astype(F32)
            total = total + jnp.where(even, landed[h][t].astype(F32), 0.0)
            held[h][results + t] = total.astype(BF16)
        store(h, i).start()

    @pl.loop(0, steps)
    def _(i):
        @pl.when(i < steps - WINDOW)
        def _():
            start_own(0, i + WINDOW)

        @pl.when(i >= steps - WINDOW)
        def _():
            start_own(1, i + WINDOW - steps)

        relay(0, i)

        for d in range(CHUNK):
            b = i * CHUNK + d
            white_t[b] = white[b].T
            for k in range(width):
                krig_t[b * width + k] = krig[b, :, k * points : (k + 1) * points].T

        @pl.loop(0, targets)
        def _(u):
            t = i * targets + u
            found = jnp.int32(refs)
            for j in range(refs):
                found = jnp.where(places[j] == t, j, found)
            inverse[t] = found

        relay_near(0, i)

    arrived(0)

    @pl.loop(0, half_steps)
    def _(q):
        @pl.when(q < steps - WINDOW)
        def _():
            start_own(1, q + WINDOW)

        relay(1, q)
        compute(0, 2 * q)
        relay_near(1, q)
        compute(0, 2 * q + 1)

    sent(0)

    @pl.loop(0, half_steps)
    def _(q):
        @pl.when(q + half_steps < steps - WINDOW)
        def _():
            start_own(1, q + half_steps + WINDOW)

        relay(1, q + half_steps)
        return_step(0, q)
        relay_near(1, q + half_steps)

    return_end(0)
    arrived(1)

    @pl.loop(0, half_steps)
    def _(q):
        compute(1, 2 * q)
        compute(1, 2 * q + 1)

        @pl.when(odd)
        def _():
            add_deep(0, q, True)

    sent(1)

    @pl.loop(0, half_steps)
    def _(q):
        return_step(1, q)

        @pl.when(odd)
        def _():
            add_deep(0, q + half_steps, True)

    return_end(1)

    @pl.loop(0, steps)
    def _(i):
        offer(0, 0, i)
        offer(1, 0, i)

    @pl.loop(0, steps)
    def _(i):
        @pl.when(odd)
        def _():
            add_deep(1, i, True)

        finish(0, i)

    @pl.loop(0, steps)
    def _(i):
        finish(1, i)

    @pl.loop(0, steps)
    def _(i):
        for h in range(2):
            for which in range(3):
                swap(h, which, i).wait_send()
            low(h, i).wait_send()
            deep(h, i).wait_send()
            store(h, i).wait()


def body(regions, fields, kriging, whitening, neighbours, home):
    blocks, points, order = kriging.shape
    series = fields.shape[1]
    region = 2 * blocks
    refs = neighbours.size
    steps = blocks // CHUNK
    any_space = pl.BlockSpec(memory_space=pl.ANY)
    smem = pl.BlockSpec(memory_space=pltpu.SMEM)
    dma = pltpu.SemaphoreType.DMA

    def rows(count):
        return pltpu.VMEM((count, points, series // 2), BF16)

    def halves(count):
        return pltpu.VMEM((2, count, points, series // 2), BF16)

    result = pl.pallas_call(
        functools.partial(kernel, regions),
        out_shape=jax.ShapeDtypeStruct((blocks, points, series), BF16),
        in_specs=[any_space, any_space, any_space, smem, smem],
        out_specs=any_space,
        scratch_shapes=[
            rows(3 * region), rows(3 * region),
            pltpu.VMEM((blocks, points, order), BF16),
            pltpu.VMEM((blocks, points, points), BF16),
            pltpu.VMEM((refs, points, points), BF16),
            pltpu.VMEM((blocks, points, points), BF16),
            rows(refs + 1), rows(refs + 1),
            halves(blocks),
            halves(3 * blocks),
            halves(2 * blocks),
            pltpu.SMEM((refs,), jnp.int32),
            pltpu.SMEM((3 * region,), jnp.int32),
            dma((4,)),
            dma((2 * steps,)), dma((2 * steps,)), dma((2 * steps,)), dma((2 * steps,)),
            dma((2,)), dma((2,)),
            dma((4 * steps,)), dma((4 * steps,)),
            dma((6 * steps,)), dma((6 * steps,)),
            dma((2 * steps,)), dma((2 * steps,)), dma((2 * steps,)), dma((2 * steps,)),
            dma((2 * steps,)),
        ],
        compiler_params=pltpu.CompilerParams(
            collective_id=0, has_side_effects=True, vmem_limit_bytes=56 * 1024 * 1024
        ),
        cost_estimate=pl.CostEstimate(
            flops=4 * blocks * points * series * (order + points),
            bytes_accessed=2 * (kriging.size + whitening.size + 2 * fields.size),
            transcendentals=0,
        ),
    )(fields.reshape(blocks, points, series), kriging, whitening, neighbours.T, home)
    return result.reshape(blocks * points, series)


def solution(mesh):
    return jax.shard_map(
        functools.partial(body, mesh.shape["space"]),
        mesh=mesh,
        in_specs=(
            P(("space", "sub"), None),
            P(("space", "sub"), None, None),
            P(("space", "sub"), None, None),
            P(("space", "sub"), None),
            P(),
        ),
        out_specs=P(("space", "sub"), None),
        check_vma=False,
    )
```

time: 128 us -> 120 us (0.938)
  Pallas kernels: 123 us -> 117 us
  local copies, waits for them, and re-layouts: 4.4 us -> 3.05 us
    pallas_call x1, Pallas kernels: 123 us -> 117 us  [body(): pl.pallas_call(functools.partial(kernel, regions), out_shape=jax.ShapeDty...]
    unnamed x2 -> x1, local copies, waits for them, and re-layouts: 4.4 us -> 3.05 us
where the time goes in v2:
time: 120 us
  Pallas kernels  117 us (98%)
  local copies, waits for them, and re-layouts  3.05 us (3%)
    pallas_call x1, Pallas kernels, body(): pl.pallas_call(functools.partial(kernel, regions), out_shape=jax.ShapeDty...  117 us
    unnamed x1, local copies, waits for them, and re-layouts  3.05 us

profile of v2, /device:TPU:2, one launch (start us, length us, event | category | flops | bytes accessed | tf_op | source)
XLA Modules:
  0.0 119.6 jit_solution(10406365291252188031)
XLA Ops:
  0.0 116.6 %shard_map.55 = bf16[16,256,256]{2,1,0:T(8,128)(2,1)} custom-call(bf16[16,256,256]{2,1,0:T(8,128)(2,1)} %bitcast.4, bf16[16,256,768]{2,1,0:T(8,128)(2,1)} %kriging.1, bf16[16,256,256]{2,1,0:T(8,128)(2,1)} %whitening.1, s32[3,16]{1,0:T(4,128)} %bitcast.5, s32[512]{0:T(512)} %home.1), custom_call_target="tpu_custom_call" | custom-call | flops 4294967296 | bytes 12582912 | tf_op jit(solution)/shard_map/pallas_call | solution.py:389
  116.6 3.0 %copy.7 = bf16[4096,256]{1,0:T(8,128)(2,1)} copy(bf16[4096,256]{1,0:T(8,128)(2,1)} %bitcast.3) | data formatting | bytes 4194304

commit v3 on v2

--- a/solution.py
+++ b/solution.py
@@ -10,8 +10,10 @@
 MESH = pl.DeviceIdType.MESH
 F32 = jnp.float32
 BF16 = jnp.bfloat16
-CHUNK = 2
-WINDOW = 4
+CHUNK = 1
+WINDOW = 8
+GROUP = 2
+EARLY = 2
 
 
 def kernel(
@@ -160,7 +162,7 @@
         return jnp.dot(a, b, preferred_element_type=F32)
 
     def compute(h, g):
-        group = [g * CHUNK + d for d in range(CHUNK)]
+        group = [g * GROUP + d for d in range(GROUP)]
         preds = []
         for b in group:
             total = None
@@ -303,9 +305,8 @@
             start_own(1, q + WINDOW)
 
         relay(1, q)
-        compute(0, 2 * q)
+        compute(0, q)
         relay_near(1, q)
-        compute(0, 2 * q + 1)
 
     sent(0)
 
@@ -320,16 +321,21 @@
         relay_near(1, q + half_steps)
 
     return_end(0)
+
+    @pl.when(odd)
+    def _():
+        for j in range(EARLY):
+            add_deep(0, j, True)
+
     arrived(1)
 
     @pl.loop(0, half_steps)
     def _(q):
-        compute(1, 2 * q)
-        compute(1, 2 * q + 1)
+        compute(1, q)
 
         @pl.when(odd)
         def _():
-            add_deep(0, q, True)
+            add_deep(0, q + EARLY, True)
 
     sent(1)
 
@@ -337,11 +343,13 @@
     def _(q):
         return_step(1, q)
 
-        @pl.when(odd)
-        def _():
-            add_deep(0, q + half_steps, True)
-
     return_end(1)
+
+    @pl.when(odd)
+    def _():
+        @pl.loop(half_steps + EARLY, steps)
+        def _(i):
+            add_deep(0, i, True)
 
     @pl.loop(0, steps)
     def _(i):

time: 120 us -> 121 us (level)
  no operation moved by 1% of the time
where the time goes in v3:
time: 121 us
  Pallas kernels  118 us (98%)
  local copies, waits for them, and re-layouts  3.05 us (3%)
    pallas_call x1, Pallas kernels, body(): pl.pallas_call(functools.partial(kernel, regions), out_shape=jax.ShapeDty...  118 us
    unnamed x1, local copies, waits for them, and re-layouts  3.05 us

profile of v3, /device:TPU:2, one launch (start us, length us, event | category | flops | bytes accessed | tf_op | source)
XLA Modules:
  0.0 120.6 jit_solution(1423208319687893882)
XLA Ops:
  0.0 117.6 %shard_map.55 = bf16[16,256,256]{2,1,0:T(8,128)(2,1)} custom-call(bf16[16,256,256]{2,1,0:T(8,128)(2,1)} %bitcast.4, bf16[16,256,768]{2,1,0:T(8,128)(2,1)} %kriging.1, bf16[16,256,256]{2,1,0:T(8,128)(2,1)} %whitening.1, s32[3,16]{1,0:T(4,128)} %bitcast.5, s32[512]{0:T(512)} %home.1), custom_call_target="tpu_custom_call" | custom-call | flops 4294967296 | bytes 12582912 | tf_op jit(solution)/shard_map/pallas_call | solution.py:397
  117.6 3.0 %copy.7 = bf16[4096,256]{1,0:T(8,128)(2,1)} copy(bf16[4096,256]{1,0:T(8,128)(2,1)} %bitcast.3) | data formatting | bytes 4194304

commit v4 on v3

--- a/solution.py
+++ b/solution.py
@@ -10,10 +10,9 @@
 MESH = pl.DeviceIdType.MESH
 F32 = jnp.float32
 BF16 = jnp.bfloat16
-CHUNK = 1
-WINDOW = 8
+CHUNK = 2
 GROUP = 2
-EARLY = 2
+EARLY = 1
 
 
 def kernel(
@@ -104,8 +103,11 @@
             near(h, i, 0).start()
 
     load_fields(0).wait()
-    for i in range(WINDOW):
+
+    @pl.loop(0, steps)
+    def _(i):
         start_own(0, i)
+
     own(0, mine).start()
     load_fields(1).wait()
     own(1, mine).start()
@@ -270,14 +272,7 @@
 
     @pl.loop(0, steps)
     def _(i):
-        @pl.when(i < steps - WINDOW)
-        def _():
-            start_own(0, i + WINDOW)
-
-        @pl.when(i >= steps - WINDOW)
-        def _():
-            start_own(1, i + WINDOW - steps)
-
+        start_own(1, i)
         relay(0, i)
 
         for d in range(CHUNK):
@@ -300,22 +295,15 @@
 
     @pl.loop(0, half_steps)
     def _(q):
-        @pl.when(q < steps - WINDOW)
-        def _():
-            start_own(1, q + WINDOW)
-
         relay(1, q)
-        compute(0, q)
+        compute(0, 2 * q)
         relay_near(1, q)
+        compute(0, 2 * q + 1)
 
     sent(0)
 
     @pl.loop(0, half_steps)
     def _(q):
-        @pl.when(q + half_steps < steps - WINDOW)
-        def _():
-            start_own(1, q + half_steps + WINDOW)
-
         relay(1, q + half_steps)
         return_step(0, q)
         relay_near(1, q + half_steps)
@@ -331,7 +319,8 @@
 
     @pl.loop(0, half_steps)
     def _(q):
-        compute(1, q)
+        compute(1, 2 * q)
+        compute(1, 2 * q + 1)
 
         @pl.when(odd)
         def _():

time: 121 us -> 122 us (level)
    pallas_call x1, Pallas kernels: 118 us -> 119 us  [body(): pl.pallas_call(functools.partial(kernel, regions), out_shape=jax.ShapeDty...]
where the time goes in v4:
time: 122 us
  Pallas kernels  119 us (98%)
  local copies, waits for them, and re-layouts  3.05 us (2%)
    pallas_call x1, Pallas kernels, body(): pl.pallas_call(functools.partial(kernel, regions), out_shape=jax.ShapeDty...  119 us
    unnamed x1, local copies, waits for them, and re-layouts  3.05 us

profile of v4, /device:TPU:2, one launch (start us, length us, event | category | flops | bytes accessed | tf_op | source)
XLA Modules:
  0.0 122.0 jit_solution(11540166303948110346)
XLA Ops:
  0.0 119.0 %shard_map.55 = bf16[16,256,256]{2,1,0:T(8,128)(2,1)} custom-call(bf16[16,256,256]{2,1,0:T(8,128)(2,1)} %bitcast.4, bf16[16,256,768]{2,1,0:T(8,128)(2,1)} %kriging.1, bf16[16,256,256]{2,1,0:T(8,128)(2,1)} %whitening.1, s32[3,16]{1,0:T(4,128)} %bitcast.5, s32[512]{0:T(512)} %home.1), custom_call_target="tpu_custom_call" | custom-call | flops 4294967296 | bytes 12582912 | tf_op jit(solution)/shard_map/pallas_call | solution.py:386
  119.0 3.0 %copy.7 = bf16[4096,256]{1,0:T(8,128)(2,1)} copy(bf16[4096,256]{1,0:T(8,128)(2,1)} %bitcast.3) | data formatting | bytes 4194304

commit v5 on v4

--- a/solution.py
+++ b/solution.py
@@ -54,28 +54,33 @@
         )
 
     def piece(ref, h, base, i):
+        if i is None:
+            return ref[h].at[pl.ds(base, blocks)]
         return ref[h].at[pl.ds(base + i * CHUNK, CHUNK)]
 
-    def far(h, i):
-        k = h * steps + i
+    def at(h, i):
+        return h * steps + (0 if i is None else i)
+
+    def far(h, i=None):
+        k = at(h, i)
         return send(
-            piece(held, h, mine, i), piece(held, h, 2 * region + mine, i), far_s.at[k], far_r.at[k], (ahead, core)
-        )
-
-    def near(h, i, start):
-        k = h * steps + i
+            piece(held, h, mine, i), piece(held, h, 2 * region + mine, i), far_s.at[h], far_r.at[k], (ahead, core)
+        )
+
+    def near(h, i=None, start=0):
+        k = at(h, i)
         return send(
             piece(held, h, start + mine, i), piece(held, h, region + mine, i),
-            near_s.at[k], near_r.at[k], (flip, core),
+            near_s.at[h], near_r.at[k], (flip, core),
         )
 
     def own(h, half):
         spot = held[h].at[pl.ds(half, blocks)]
         return send(spot, spot, own_s.at[h], own_r.at[h], partner)
 
-    def handed(h, which, half, i):
+    def handed(h, which, half, i=None):
         spot = piece(held, h, which * region + half, i)
-        k = (h * 2 + which - 1) * steps + i
+        k = h * 2 + which - 1
         return send(spot, spot, pass_s.at[k], pass_r.at[k], partner)
 
     def load_fields(h):
@@ -144,21 +149,15 @@
 
     def arrived(h):
         own(h, theirs).wait_recv()
-
-        @pl.loop(0, steps)
-        def _(i):
-            handed(h, 2, theirs, i).wait_recv()
-            handed(h, 1, theirs, i).wait_recv()
+        handed(h, 2, theirs).wait_recv()
+        handed(h, 1, theirs).wait_recv()
 
     def sent(h):
         own(h, mine).wait_send()
-
-        @pl.loop(0, steps)
-        def _(i):
-            far(h, i).wait_send()
-            near(h, i, 0).wait_send()
-            handed(h, 2, mine, i).wait_send()
-            handed(h, 1, mine, i).wait_send()
+        far(h).wait_send()
+        near(h).wait_send()
+        handed(h, 2, mine).wait_send()
+        handed(h, 1, mine).wait_send()
 
     def dot(a, b):
         return jnp.dot(a, b, preferred_element_type=F32)
@@ -181,30 +180,33 @@
             for k in range(width):
                 back[h][b * width + k] = dot(krig_t[b * width + k], p).astype(BF16)
 
-    def swap(h, which, i):
-        k = (h * 3 + which) * steps + i
+    def swap(h, which, i=None):
+        k = (h * 3 + which) * steps + (0 if i is None else i)
         return send(
             piece(held, h, which * blocks, i), piece(swapped, h, which * blocks, i),
-            swap_s.at[k], swap_r.at[k], partner,
-        )
-
-    def offer(h, which, i):
+            swap_s.at[h * 3 + which], swap_r.at[k], partner,
+        )
+
+    def stage(h, which, i):
         for d in range(CHUNK):
             t = i * CHUNK + d
             held[h][which * blocks + t] = back[h][inverse[which * region + theirs + t]]
+
+    def offer(h, which, i):
+        stage(h, which, i)
         swap(h, which, i).start()
 
     sums = 3 * blocks
     results = sums + 2 * blocks
 
-    def low(h, i):
-        k = h * steps + i
-        return send(piece(held, h, sums, i), piece(landed, h, 0, i), low_s.at[k], low_r.at[k], (flip, core))
-
-    def deep(h, i):
-        k = h * steps + i
+    def low(h, i=None):
+        k = at(h, i)
+        return send(piece(held, h, sums, i), piece(landed, h, 0, i), low_s.at[h], low_r.at[k], (flip, core))
+
+    def deep(h, i=None):
+        k = at(h, i)
         return send(
-            piece(held, h, sums + blocks, i), piece(landed, h, blocks, i), deep_s.at[k], deep_r.at[k], (behind, core)
+            piece(held, h, sums + blocks, i), piece(landed, h, blocks, i), deep_s.at[h], deep_r.at[k], (behind, core)
         )
 
     def add_low(h, i):
@@ -248,16 +250,13 @@
         for e in range(2):
             add(h, steps - 2 + e)
 
-    def store(h, i):
+    def store(h, i=None):
+        spots = pl.ds(0, blocks) if i is None else pl.ds(i * CHUNK, CHUNK)
         return pltpu.make_async_copy(
-            piece(held, h, results, i),
-            out.at[pl.ds(i * CHUNK, CHUNK), :, pl.ds(h * cols, cols)],
-            out_sem.at[h * steps + i],
+            piece(held, h, results, i), out.at[spots, :, pl.ds(h * cols, cols)], out_sem.at[h]
         )
 
     def finish(h, i):
-        swap(h, 0, i).wait_recv()
-
         @pl.when(even)
         def _():
             low(h, i).wait_recv()
@@ -342,8 +341,12 @@
 
     @pl.loop(0, steps)
     def _(i):
-        offer(0, 0, i)
-        offer(1, 0, i)
+        stage(0, 0, i)
+        stage(1, 0, i)
+
+    swap(0, 0).start()
+    swap(1, 0).start()
+    swap(0, 0).wait_recv()
 
     @pl.loop(0, steps)
     def _(i):
@@ -353,18 +356,21 @@
 
         finish(0, i)
 
+    for which in range(3):
+        swap(0, which).wait_send()
+        swap(1, which).wait_send()
+    swap(1, 0).wait_recv()
+    low(0).wait_send()
+    deep(0).wait_send()
+    store(0).wait()
+
     @pl.loop(0, steps)
     def _(i):
         finish(1, i)
 
-    @pl.loop(0, steps)
-    def _(i):
-        for h in range(2):
-            for which in range(3):
-                swap(h, which, i).wait_send()
-            low(h, i).wait_send()
-            deep(h, i).wait_send()
-            store(h, i).wait()
+    low(1).wait_send()
+    deep(1).wait_send()
+    store(1).wait()
 
 
 def body(regions, fields, kriging, whitening, neighbours, home):
@@ -385,7 +391,7 @@
 
     result = pl.pallas_call(
         functools.partial(kernel, regions),
-        out_shape=jax.ShapeDtypeStruct((blocks, points, series), BF16),
+        out_shape=jax.ShapeDtypeStruct((blocks + 1, points, series), BF16),
         in_specs=[any_space, any_space, any_space, smem, smem],
         out_specs=any_space,
         scratch_shapes=[
@@ -401,12 +407,12 @@
             pltpu.SMEM((refs,), jnp.int32),
             pltpu.SMEM((3 * region,), jnp.int32),
             dma((4,)),
-            dma((2 * steps,)), dma((2 * steps,)), dma((2 * steps,)), dma((2 * steps,)),
+            dma((2,)), dma((2 * steps,)), dma((2,)), dma((2 * steps,)),
             dma((2,)), dma((2,)),
-            dma((4 * steps,)), dma((4 * steps,)),
-            dma((6 * steps,)), dma((6 * steps,)),
-            dma((2 * steps,)), dma((2 * steps,)), dma((2 * steps,)), dma((2 * steps,)),
-            dma((2 * steps,)),
+            dma((4,)), dma((4,)),
+            dma((6,)), dma((6 * steps,)),
+            dma((2,)), dma((2 * steps,)), dma((2,)), dma((2 * steps,)),
+            dma((2,)),
         ],
         compiler_params=pltpu.CompilerParams(
             collective_id=0, has_side_effects=True, vmem_limit_bytes=56 * 1024 * 1024
@@ -417,7 +423,7 @@
             transcendentals=0,
         ),
     )(fields.reshape(blocks, points, series), kriging, whitening, neighbours.T, home)
-    return result.reshape(blocks * points, series)
+    return result[:blocks].reshape(blocks * points, series)
 
 
 def solution(mesh):

time: 122 us -> 121 us (level)
  Pallas kernels: 119 us -> 117 us
    slice x0 -> x1, local copies, waits for them, and re-layouts: none -> 3.1 us  [body(): return result[:blocks].reshape(blocks * points, series)]
    unnamed x1 -> x0, local copies, waits for them, and re-layouts: 3.05 us -> none
    pallas_call x1, Pallas kernels: 119 us -> 117 us  [body(): pl.pallas_call(functools.partial(kernel, regions), out_shape=jax.ShapeDty...]
where the time goes in v5:
time: 121 us; the launch traced here: 120 us
  Pallas kernels  117 us (97%)
  local copies, waits for them, and re-layouts  3.1 us (3%)
    pallas_call x1, Pallas kernels, body(): pl.pallas_call(functools.partial(kernel, regions), out_shape=jax.ShapeDty...  117 us
    slice x1, local copies, waits for them, and re-layouts, body(): return result[:blocks].reshape(blocks * points, series)  3.1 us

profile of v5, /device:TPU:2, one launch (start us, length us, event | category | flops | bytes accessed | tf_op | source)
XLA Modules:
  0.0 120.5 jit_solution(11993290197848119713)
XLA Ops:
  0.0 117.4 %shard_map.55 = bf16[17,256,256]{2,1,0:T(8,128)(2,1)} custom-call(bf16[16,256,256]{2,1,0:T(8,128)(2,1)} %bitcast.3, bf16[16,256,768]{2,1,0:T(8,128)(2,1)} %kriging.1, bf16[16,256,256]{2,1,0:T(8,128)(2,1)} %whitening.1, s32[3,16]{1,0:T(4,128)} %bitcast.4, s32[512]{0:T(512)} %home.1), custom_call_target="tpu_custom_call" | custom-call | flops 4294967296 | bytes 12582912 | tf_op jit(solution)/shard_map/pallas_call | solution.py:392
  117.4 3.1 %slice.3 = bf16[16,256,256]{2,1,0:T(8,128)(2,1)} slice(bf16[17,256,256]{2,1,0:T(8,128)(2,1)} %shard_map.55), slice={[0:16], [0:256], [0:256]} | slice | bytes 4194304 | tf_op jit(solution)/shard_map/slice | solution.py:426

commit v6 on v5

--- a/solution.py
+++ b/solution.py
@@ -11,6 +11,7 @@
 F32 = jnp.float32
 BF16 = jnp.bfloat16
 CHUNK = 2
+OUTWARD = 1
 GROUP = 2
 EARLY = 1
 
@@ -35,6 +36,8 @@
     refs = blocks * width
     steps = blocks // CHUNK
     half_steps = steps // 2
+    hops = blocks // OUTWARD
+    quarter = hops // half_steps // 2
     me = lax.axis_index("space")
     core = lax.axis_index("sub")
     other = 1 - core
@@ -58,19 +61,27 @@
             return ref[h].at[pl.ds(base, blocks)]
         return ref[h].at[pl.ds(base + i * CHUNK, CHUNK)]
 
+    def part(h, base, i):
+        if i is None:
+            return held[h].at[pl.ds(base, blocks)]
+        return held[h].at[pl.ds(base + i * OUTWARD, OUTWARD)]
+
     def at(h, i):
         return h * steps + (0 if i is None else i)
 
+    def hop(h, i):
+        return h * hops + (0 if i is None else i)
+
     def far(h, i=None):
-        k = at(h, i)
+        k = hop(h, i)
         return send(
-            piece(held, h, mine, i), piece(held, h, 2 * region + mine, i), far_s.at[h], far_r.at[k], (ahead, core)
+            part(h, mine, i), part(h, 2 * region + mine, i), far_s.at[h], far_r.at[k], (ahead, core)
         )
 
     def near(h, i=None, start=0):
-        k = at(h, i)
+        k = hop(h, i)
         return send(
-            piece(held, h, start + mine, i), piece(held, h, region + mine, i),
+            part(h, start + mine, i), part(h, region + mine, i),
             near_s.at[h], near_r.at[k], (flip, core),
         )
 
@@ -79,7 +90,7 @@
         return send(spot, spot, own_s.at[h], own_r.at[h], partner)
 
     def handed(h, which, half, i=None):
-        spot = piece(held, h, which * region + half, i)
+        spot = part(h, which * region + half, i)
         k = h * 2 + which - 1
         return send(spot, spot, pass_s.at[k], pass_r.at[k], partner)
 
@@ -109,7 +120,7 @@
 
     load_fields(0).wait()
 
-    @pl.loop(0, steps)
+    @pl.loop(0, hops)
     def _(i):
         start_own(0, i)
 
@@ -132,7 +143,7 @@
 
     load_w.wait()
     load_k.wait()
-    targets = 3 * region // steps
+    targets = 3 * region // hops
 
     def relay(h, i):
         far(h, i).wait_recv()
@@ -269,13 +280,13 @@
             held[h][results + t] = total.astype(BF16)
         store(h, i).start()
 
-    @pl.loop(0, steps)
+    @pl.loop(0, hops)
     def _(i):
         start_own(1, i)
         relay(0, i)
 
-        for d in range(CHUNK):
-            b = i * CHUNK + d
+        for d in range(OUTWARD):
+            b = i * OUTWARD + d
             white_t[b] = white[b].T
             for k in range(width):
                 krig_t[b * width + k] = krig[b, :, k * points : (k + 1) * points].T
@@ -294,18 +305,21 @@
 
     @pl.loop(0, half_steps)
     def _(q):
-        relay(1, q)
-        compute(0, 2 * q)
-        relay_near(1, q)
-        compute(0, 2 * q + 1)
+        for e in range(quarter):
+            relay(1, q * quarter + e)
+            compute(0, 2 * q + e)
+            relay_near(1, q * quarter + e)
 
     sent(0)
 
     @pl.loop(0, half_steps)
     def _(q):
-        relay(1, q + half_steps)
-        return_step(0, q)
-        relay_near(1, q + half_steps)
+        for e in range(quarter):
+            k = (half_steps + q) * quarter + e
+            relay(1, k)
+            if e == 0:
+                return_step(0, q)
+            relay_near(1, k)
 
     return_end(0)
 
@@ -379,6 +393,7 @@
     region = 2 * blocks
     refs = neighbours.size
     steps = blocks // CHUNK
+    hops = blocks // OUTWARD
     any_space = pl.BlockSpec(memory_space=pl.ANY)
     smem = pl.BlockSpec(memory_space=pltpu.SMEM)
     dma = pltpu.SemaphoreType.DMA
@@ -391,7 +406,7 @@
 
     result = pl.pallas_call(
         functools.partial(kernel, regions),
-        out_shape=jax.ShapeDtypeStruct((blocks + 1, points, series), BF16),
+        out_shape=jax.ShapeDtypeStruct((blocks, points, series), BF16),
         in_specs=[any_space, any_space, any_space, smem, smem],
         out_specs=any_space,
         scratch_shapes=[
@@ -407,7 +422,7 @@
             pltpu.SMEM((refs,), jnp.int32),
             pltpu.SMEM((3 * region,), jnp.int32),
             dma((4,)),
-            dma((2,)), dma((2 * steps,)), dma((2,)), dma((2 * steps,)),
+            dma((2,)), dma((2 * hops,)), dma((2,)), dma((2 * hops,)),
             dma((2,)), dma((2,)),
             dma((4,)), dma((4,)),
             dma((6,)), dma((6 * steps,)),
@@ -423,7 +438,7 @@
             transcendentals=0,
         ),
     )(fields.reshape(blocks, points, series), kriging, whitening, neighbours.T, home)
-    return result[:blocks].reshape(blocks * points, series)
+    return result.reshape(blocks * points, series)
 
 
 def solution(mesh):

time: 121 us -> 118 us (0.975)
  Pallas kernels: 117 us -> 114 us
    slice x1 -> x0, local copies, waits for them, and re-layouts: 3.1 us -> none  [body(): return result[:blocks].reshape(blocks * points, series)]
    pallas_call x1, Pallas kernels: 117 us -> 114 us  [body(): pl.pallas_call(functools.partial(kernel, regions), out_shape=jax.ShapeDty...]
    unnamed x0 -> x1, local copies, waits for them, and re-layouts: none -> 3.05 us
where the time goes in v6:
time: 118 us; the launch traced here: 117 us
  Pallas kernels  114 us (97%)
  local copies, waits for them, and re-layouts  3.05 us (3%)
    pallas_call x1, Pallas kernels, body(): pl.pallas_call(functools.partial(kernel, regions), out_shape=jax.ShapeDty...  114 us
    unnamed x1, local copies, waits for them, and re-layouts  3.05 us

profile of v6, /device:TPU:2, one launch (start us, length us, event | category | flops | bytes accessed | tf_op | source)
XLA Modules:
  0.0 117.4 jit_solution(5460512218140690299)
XLA Ops:
  0.0 114.3 %shard_map.55 = bf16[16,256,256]{2,1,0:T(8,128)(2,1)} custom-call(bf16[16,256,256]{2,1,0:T(8,128)(2,1)} %bitcast.4, bf16[16,256,768]{2,1,0:T(8,128)(2,1)} %kriging.1, bf16[16,256,256]{2,1,0:T(8,128)(2,1)} %whitening.1, s32[3,16]{1,0:T(4,128)} %bitcast.5, s32[512]{0:T(512)} %home.1), custom_call_target="tpu_custom_call" | custom-call | flops 4294967296 | bytes 12582912 | tf_op jit(solution)/shard_map/pallas_call | solution.py:407
  114.3 3.0 %copy.7 = bf16[4096,256]{1,0:T(8,128)(2,1)} copy(bf16[4096,256]{1,0:T(8,128)(2,1)} %bitcast.3) | data formatting | bytes 4194304

commit v7 on v6

--- a/solution.py
+++ b/solution.py
@@ -126,6 +126,11 @@
 
     own(0, mine).start()
     load_fields(1).wait()
+
+    @pl.loop(0, hops)
+    def _(i):
+        start_own(1, i)
+
     own(1, mine).start()
 
     for h in range(2):
@@ -282,7 +287,6 @@
 
     @pl.loop(0, hops)
     def _(i):
-        start_own(1, i)
         relay(0, i)
 
         for d in range(OUTWARD):

time: 118 us -> 118 us (level)
  no operation moved by 1% of the time
where the time goes in v7:
time: 118 us; the launch traced here: 117 us
  Pallas kernels  114 us (97%)
  local copies, waits for them, and re-layouts  3.05 us (3%)
    pallas_call x1, Pallas kernels, body(): pl.pallas_call(functools.partial(kernel, regions), out_shape=jax.ShapeDty...  114 us
    unnamed x1, local copies, waits for them, and re-layouts  3.05 us

profile of v7, /device:TPU:2, one launch (start us, length us, event | category | flops | bytes accessed | tf_op | source)
XLA Modules:
  0.0 117.4 jit_solution(11671858873648138808)
XLA Ops:
  0.0 114.3 %shard_map.55 = bf16[16,256,256]{2,1,0:T(8,128)(2,1)} custom-call(bf16[16,256,256]{2,1,0:T(8,128)(2,1)} %bitcast.4, bf16[16,256,768]{2,1,0:T(8,128)(2,1)} %kriging.1, bf16[16,256,256]{2,1,0:T(8,128)(2,1)} %whitening.1, s32[3,16]{1,0:T(4,128)} %bitcast.5, s32[512]{0:T(512)} %home.1), custom_call_target="tpu_custom_call" | custom-call | flops 4294967296 | bytes 12582912 | tf_op jit(solution)/shard_map/pallas_call | solution.py:411
  114.3 3.0 %copy.7 = bf16[4096,256]{1,0:T(8,128)(2,1)} copy(bf16[4096,256]{1,0:T(8,128)(2,1)} %bitcast.3) | data formatting | bytes 4194304
